TPU v7x, 32 devices: a whole 2x2x4 slice. The times are simulated.
32 devices in a mesh: parts: 2 (over x), src: 16 (over z, y, core).
Axes of the slice: x: 2, y: 2, z: 4, core: 2. Of those that a mesh axis runs over, the one named last changes fastest.
Arguments:
- estimate: bfloat16 [64, 32, 1024], P(('parts', 'src')), parts along dimension 0, may hold values from -64 to 64
- records: bfloat16 [8, 32, 1152], P('parts', 'src'), parts along dimension 0, may hold values from -64 to 64
- dip_receiver: bfloat16 [64, 32, 1024], P(('parts', 'src')), parts along dimension 0, may hold values from -1 to 1
- dip_source: bfloat16 [64, 32, 1024], P(('parts', 'src')), parts along dimension 0, may hold values from -1 to 1
- delays: int32 [64], P('parts'), parts along dimension 0, may hold values from 0 to 128
- boat: int32 [64], P('parts'), parts along dimension 0, may hold values from 0 to 3
- pair: int32 [64], P('parts'), parts along dimension 0, may hold values from 0 to 31, as said below
Outputs:
- refined: bfloat16 [64, 32, 1024], P(('parts', 'src')), parts along dimension 0
There are 2 independent parts, one for each index of `parts`. A program takes and returns all parts, laid end to end along the dimension named above; each array names one. Nothing has to cross between parts.
Inputs may be any that keep to these rules, and one draw needn't show every extreme that they name: pair is a permutation that maps each aligned block of 2 indices onto itself.
All inputs are finite; a program needn't handle non-finite values.
Results may differ from a plain program's by a relative error of at most 0.015.
Values may be sent and summed in bfloat16 or wider, within the bound.
A program may use at most 64 MiB of HBM per device.

v0:
```python
import jax
import jax.numpy as jnp
from jax import lax
from jax.sharding import PartitionSpec as P

WBLK = 256
ITERS = 2


step_size = 0.0625
filter_weight = 0.25
shrink_ratio = 0.3
HALF_ROOT = 0.7071067811865476


def passed_along(value, axis, steps):
    count = lax.axis_size(axis)
    leading, last = (max(0, -steps), min(count, count - steps))
    return lax.ppermute(value, axis, [(source, source + steps) for source in range(leading, last)])


def haar_matrix(length):
    matrix = jnp.ones((1, 1), jnp.float32)
    while matrix.shape[0] < length:
        previous = matrix.shape[0]
        coarser = jnp.kron(matrix, jnp.ones((1, 2), jnp.float32))
        finest = jnp.kron(
            jnp.eye(previous, dtype=jnp.float32), jnp.array([[1.0, -1.0]], jnp.float32)
        )
        matrix = jnp.concatenate([coarser, finest], axis=0) * HALF_ROOT
    return matrix


def place_trace(single, sample_lag, record_len):
    canvas = jnp.zeros((single.shape[0], record_len), single.dtype)
    return lax.dynamic_update_slice(canvas, single, (jnp.zeros((), jnp.int32), sample_lag))


def cut_trace(row_data, sample_lag, samples):
    return lax.dynamic_slice(
        row_data, (jnp.zeros((), jnp.int32), sample_lag), (row_data.shape[0], samples)
    )


def predict(prior, dip_field):
    zero_column = jnp.zeros_like(prior[..., :1])
    earlier = jnp.concatenate([zero_column, prior[..., :-1]], axis=-1)
    later = jnp.concatenate([prior[..., 1:], zero_column], axis=-1)
    return (
        earlier * dip_field * (dip_field + 1.0) * 0.5
        + prior * (1.0 - dip_field * dip_field)
        + later * dip_field * (dip_field - 1.0) * 0.5
    )


def body(estimate, records, dip_receiver, dip_source, delays, boat, pair):
    local_src, receivers, samples = estimate.shape
    total_src = delays.shape[0]
    record_count, local_recv, record_len = records.shape
    cell_count = total_src * receivers * samples
    haar_table = haar_matrix(WBLK)
    offset = lax.axis_index("src") * local_src
    local_pair = lax.dynamic_slice_in_dim(pair, offset, local_src) - offset
    onehot = (boat[None, :] == jnp.arange(record_count, dtype=jnp.int32)[:, None]).astype(
        jnp.bfloat16
    )
    records_wide = records.astype(jnp.float32)
    receiver_dip = dip_receiver.astype(jnp.float32)
    source_dip = dip_source.astype(jnp.float32)
    current = estimate
    for iteration in range(ITERS):
        gathered = lax.all_to_all(current, "src", split_axis=1, concat_axis=0, tiled=True)
        shifted = jax.vmap(lambda single, sample_lag: place_trace(single, sample_lag, record_len))(
            gathered, delays
        )
        predicted = jnp.dot(
            onehot, shifted.reshape(total_src, -1), preferred_element_type=jnp.float32
        )
        residual = records_wide - predicted.reshape(record_count, local_recv, record_len)
        picked = jnp.take(residual, boat, axis=0)
        adjoint = jax.vmap(lambda row_data, sample_lag: cut_trace(row_data, sample_lag, samples))(
            picked, delays
        )
        update_recv = (gathered.astype(jnp.float32) + step_size * adjoint).astype(jnp.bfloat16)
        adjoint_src = lax.all_to_all(adjoint, "src", split_axis=0, concat_axis=1, tiled=True)
        update_src = (current.astype(jnp.float32) + step_size * adjoint_src).astype(jnp.bfloat16)
        partial_value = jnp.sum(jnp.square(update_src.astype(jnp.float32)))
        energy = lax.psum(partial_value, "src")
        threshold = shrink_ratio * jnp.sqrt(energy / cell_count + 1e-06)
        swapped = jnp.take(jnp.take(update_recv, pair, axis=0), local_pair, axis=1).transpose(
            1, 0, 2
        )
        symmetric = (0.5 * (update_src.astype(jnp.float32) + swapped.astype(jnp.float32))).astype(
            jnp.bfloat16
        )
        rim_row = passed_along(symmetric[-1:], "src", 1)
        sym_wide = symmetric.astype(jnp.float32)
        prior_receiver = jnp.concatenate(
            [jnp.zeros_like(sym_wide[:, :1]), sym_wide[:, :-1]], axis=1
        )
        prior_source = jnp.concatenate([rim_row, symmetric[:-1]], axis=0).astype(jnp.float32)
        filtered = sym_wide - filter_weight * (
            sym_wide
            - predict(prior_receiver, receiver_dip)
            + (sym_wide - predict(prior_source, source_dip))
        )
        coeffs = jnp.dot(
            filtered.reshape(-1, WBLK),
            haar_table.T,
            precision=lax.Precision.HIGHEST,
            preferred_element_type=jnp.float32,
        )
        shrunk = coeffs - jnp.clip(coeffs, -threshold, threshold)
        restored = jnp.dot(
            shrunk, haar_table, precision=lax.Precision.HIGHEST, preferred_element_type=jnp.float32
        )
        current = restored.reshape(local_src, receivers, samples).astype(jnp.bfloat16)
    return current


def solution(mesh):
    return jax.shard_map(
        body,
        mesh=mesh,
        in_specs=(
            P(("parts", "src"), None, None),
            P("parts", "src", None),
            P(("parts", "src"), None, None),
            P(("parts", "src"), None, None),
            P("parts"),
            P("parts"),
            P("parts"),
        ),
        out_specs=P(("parts", "src"), None, None),
        check_vma=False,
    )
```

profile of v0, /device:TPU:8, one launch (start us, length us, event | category | flops | bytes accessed | tf_op | source)
XLA Modules:
  0.0 726.6 jit_solution(8915670298121401342)
XLA Ops:
  1.7 6.3 all-to-all-start
  14.5 215.0 %while.6 = (s32[]{:T(128)}, bf16[32,2,1152]{2,1,0:T(2,128)(2,1)S(1)}, s32[32,3]{0,1:T(4,128)S(1)}, bf16[32,2,1024]{2,1,0:T(2,128)(2,1)S(1)}, s32[]{:T(128)}, /*index=5*/s32[3]{0:T(128)S(1)}, s32[]{:T(128)}) while((s32[]{:T(128)}, bf16[32,2,1152]{2,1,0:T(2,128)(2,1)S(1)}, s32[32,3]{0,1:T(4,128)S(1)}, bf16[32,2,1024]{2,1,0:T(2,128)(2,1)S(1)}, ...), condition=%wide.while_cond.2, body=%wide.while_body.2.sunk | while | flops 2067 | bytes 20651 | solution.py:36
  15.1 2.6 and_reduce_fusion.4
  21.9 2.6 and_reduce_fusion.4
  28.6 2.6 and_reduce_fusion.4
  35.3 2.6 and_reduce_fusion.4
  42.0 2.6 and_reduce_fusion.4
  48.8 2.6 and_reduce_fusion.4
  55.5 2.6 and_reduce_fusion.4
  62.2 2.6 and_reduce_fusion.4
  69.0 2.6 and_reduce_fusion.4
  75.7 2.6 and_reduce_fusion.4
  82.4 2.6 and_reduce_fusion.4
  89.1 2.6 and_reduce_fusion.4
  95.9 2.6 and_reduce_fusion.4
  102.6 2.6 and_reduce_fusion.4
  109.3 2.6 and_reduce_fusion.4
  116.1 2.6 and_reduce_fusion.4
  122.8 2.6 and_reduce_fusion.4
  129.5 2.6 and_reduce_fusion.4
  136.3 2.6 and_reduce_fusion.4
  143.0 2.6 and_reduce_fusion.4
  149.7 2.6 and_reduce_fusion.4
  156.4 2.6 and_reduce_fusion.4
  163.2 2.6 and_reduce_fusion.4
  169.9 2.6 and_reduce_fusion.4
  176.6 2.6 and_reduce_fusion.4
  183.4 2.6 and_reduce_fusion.4
  190.1 2.6 and_reduce_fusion.4
  196.8 2.6 and_reduce_fusion.4
  203.5 2.6 and_reduce_fusion.4
  210.1 2.6 and_reduce_fusion.4
  216.7 2.6 and_reduce_fusion.4
  223.4 2.6 and_reduce_fusion.4
  231.6 79.5 %while.4 = (s32[]{:T(128)}, f32[32,2,1152]{2,1,0:T(2,128)S(1)}, s32[32,3]{0,1:T(4,128)S(1)}, f32[32,2,1024]{2,1,0:T(2,128)}, s32[]{:T(128)}) while((s32[]{:T(128)}, f32[32,2,1152]{2,1,0:T(2,128)S(1)}, s32[32,3]{0,1:T(4,128)S(1)}, f32[32,2,1024]{2,1,0:T(2,128)}, s32[]{:T(128)}) %tuple.81), condition=%wide.while_cond, body=%wide.while_body.sunk | while | flops 2 | bytes 18025 | solution.py:40
  311.1 6.0 all-to-all-start.1
  319.9 5.3 all-to-all-done.1
  327.0 2.6 collective-permute-start
  329.6 24.9 %psum.14 = f32[]{:T(128)} all-reduce(f32[]{:T(128)} %get-tuple-element.92), channel_id=1, replica_groups=mesh['parts'=2,'src'=16] {'src'}, use_global_device_ids=true, to_apply=%region_2.6 | all-reduce | flops 1 | bytes 8 | tf_op jit(solution)/shard_map/psum | solution.py:88
  358.5 10.7 %all-to-all-start.2 = ((bf16[2,32,1024]{2,0,1:T(2,128)(2,1)}), bf16[2,32,1024]{2,0,1:T(2,128)(2,1)S(1)}, u32[]{:S(2)}, u32[]{:S(2)}) async-start(bf16[2,32,1024]{2,0,1:T(2,128)(2,1)} %copy.60), calls=%async_computation.2 | async-start | bytes 262144 | tf_op jit(solution)/shard_map/all_to_all | solution.py:72
  369.2 5.5 all-to-all-done.2
  374.9 214.3 %while.7 = (s32[]{:T(128)}, bf16[32,2,1152]{2,1,0:T(2,128)(2,1)S(1)}, s32[32,3]{0,1:T(4,128)S(1)}, bf16[32,2,1024]{2,1,0:T(2,128)(2,1)S(1)}, s32[]{:T(128)}, /*index=5*/s32[3]{0:T(128)S(1)}, s32[]{:T(128)}) while((s32[]{:T(128)}, bf16[32,2,1152]{2,1,0:T(2,128)(2,1)S(1)}, s32[32,3]{0,1:T(4,128)S(1)}, bf16[32,2,1024]{2,1,0:T(2,128)(2,1)S(1)}, ...), condition=%wide.while_cond.3, body=%wide.while_body.3.sunk | while | flops 2067 | bytes 20651 | solution.py:36
  422.4 2.6 and_reduce_fusion.5
  591.2 85.0 %while.5 = (s32[]{:T(128)}, f32[32,2,1152]{2,1,0:T(2,128)S(1)}, s32[32,3]{0,1:T(4,128)S(1)}, f32[32,2,1024]{2,1,0:T(2,128)}, s32[]{:T(128)}) while((s32[]{:T(128)}, f32[32,2,1152]{2,1,0:T(2,128)S(1)}, s32[32,3]{0,1:T(4,128)S(1)}, f32[32,2,1024]{2,1,0:T(2,128)}, s32[]{:T(128)}) %tuple.92), condition=%wide.while_cond.1, body=%wide.while_body.1.sunk | while | flops 2 | bytes 18025 | solution.py:40
  676.2 6.0 all-to-all-start.3
  684.9 5.1 all-to-all-done.3
  691.4 25.3 %psum.15 = f32[]{:T(128)} all-reduce(f32[]{:T(128)} %multiply_reduce_fusion), channel_id=1, replica_groups=mesh['parts'=2,'src'=16] {'src'}, use_global_device_ids=true, to_apply=%region_5.9 | all-reduce | flops 1 | bytes 8 | tf_op jit(solution)/shard_map/psum | solution.py:88
  719.5 4.9 collective-permute-done.1
  (622 shorter events, 534.5 us)
Async XLA Ops:
  1.7 12.0 %all-to-all-start = ((bf16[2,32,1024]{2,0,1:T(2,128)(2,1)}), bf16[2,32,1024]{2,0,1:T(2,128)(2,1)S(1)}, u32[]{:S(2)}, u32[]{:S(2)}) async-start(bf16[2,32,1024]{2,0,1:T(2,128)(2,1)} %copy.53), calls=%async_computation | async-start | bytes 262144 | tf_op jit(solution)/shard_map/all_to_all | solution.py:72
  8.0 0.7 copy-start.9
  8.7 0.7 copy-start.6
  9.4 0.7 copy-start.8
  10.2 0.7 copy-start.4
  10.8 0.7 copy-start.5
  13.9 0.7 copy-start.3
  14.5 215.0 %copy-start.7 = (bf16[4,2,1152]{2,1,0:T(2,128)(2,1)S(1)}, bf16[4,2,1152]{2,1,0:T(2,128)(2,1)}, u32[]{:S(2)}) copy-start(bf16[4,2,1152]{2,1,0:T(2,128)(2,1)} %param.22) | copy-start | bytes 55300
  311.1 14.2 %all-to-all-start.1 = ((f32[32,2,1024]{2,1,0:T(2,128)}), f32[32,2,1024]{2,1,0:T(2,128)S(1)}, u32[]{:S(2)}, u32[]{:S(2)}) async-start(f32[32,2,1024]{2,1,0:T(2,128)} %get-tuple-element.15), calls=%async_computation.1 | async-start | bytes 524288 | tf_op jit(solution)/shard_map/all_to_all | solution.py:85
  325.4 0.9 copy-start.2
  327.0 28.3 %collective-permute-start = (bf16[1,32,1024]{2,1,0:T(8,128)(2,1)S(1)}, bf16[1,32,1024]{2,1,0:T(8,128)(2,1)S(1)}, u32[]{:S(2)}, u32[]{:S(2)}) collective-permute-start(bf16[1,32,1024]{2,1,0:T(8,128)(2,1)S(1)} %get-tuple-element.104), channel_id=1, source_target_pairs={{0,1},{1,2},{2,3},{3,4},{4,5},{5,6},{6,7},{7,8},{8,9},{9,10},{10,1... | collective-permute-start | bytes 196616 | tf_op jit(solution)/shard_map/ppermute | solution.py:19
  355.3 0.9 copy-start
  355.4 1.0 copy-start.1
  358.5 16.1 %all-to-all-start.2 = ((bf16[2,32,1024]{2,0,1:T(2,128)(2,1)}), bf16[2,32,1024]{2,0,1:T(2,128)(2,1)S(1)}, u32[]{:S(2)}, u32[]{:S(2)}) async-start(bf16[2,32,1024]{2,0,1:T(2,128)(2,1)} %copy.60), calls=%async_computation.2 | async-start | bytes 262144 | tf_op jit(solution)/shard_map/all_to_all | solution.py:72
  676.2 13.9 %all-to-all-start.3 = ((f32[32,2,1024]{2,1,0:T(2,128)}), f32[32,2,1024]{2,1,0:T(2,128)S(1)}, u32[]{:S(2)}, u32[]{:S(2)}) async-start(f32[32,2,1024]{2,1,0:T(2,128)} %get-tuple-element.23), calls=%async_computation.3 | async-start | bytes 524288 | tf_op jit(solution)/shard_map/all_to_all | solution.py:85
  717.4 7.0 collective-permute-start.1
where the time goes:
time: 738 us; the launch traced here: 727 us
  local copies, waits for them, and re-layouts  322 us (44%)
  other arithmetic  295 us (40%)
  blocking collectives  50.2 us (7%)
  starting transfers between devices  33.5 us (5%)
  waiting for transfers between devices  20.8 us (3%)
    scatter x128, other arithmetic  288 us
    gather x192, local copies, waits for them, and re-layouts  164 us
    scatter x192, local copies, waits for them, and re-layouts  140 us
    psum x2, blocking collectives, body(): energy = lax.psum(partial_value, 'src')  50.2 us
    all_to_all x2, starting transfers between devices, body(): lax.all_to_all(current, 'src', split_axis=1, concat_axis=0, tiled=True)  17 us
  transfers between devices with their start and end apart: 6, of which 4 were waited for; matrix products, arithmetic and copies ran while one was open for 1% of the time, Pallas kernels for 0%

commit v1 on v0

v1 whole, which is shorter than its diff:
```python
import functools
import math

import jax
import jax.numpy as jnp
import numpy as np
from jax import lax
from jax.experimental import pallas as pl
from jax.experimental.pallas import tpu as pltpu
from jax.sharding import PartitionSpec as P

WBLK = 256
ITERS = 2
LANES = 128

STEP_SIZE = 0.0625
SHRINK_RATIO = 0.3

F32 = jnp.float32
BF16 = jnp.bfloat16


def haar_signs(length):
    signs = np.zeros((length, length), np.float32)
    scales = np.zeros((1, length), np.float32)
    signs[0] = 1.0
    scales[0, 0] = 1.0 / math.sqrt(length)
    row, support = 1, length
    while support > 1:
        for start in range(0, length, support):
            signs[row, start : start + support // 2] = 1.0
            signs[row, start + support // 2 : start + support] = -1.0
            scales[0, row] = 1.0 / math.sqrt(support)
            row += 1
        support //= 2
    return signs, scales


def row_orders(n, local, blocks):
    total = n * local
    size = blocks * local * total
    slab = np.zeros((size, size), np.float32)
    node = np.zeros((size, size), np.float32)
    for d in range(n):
        for w in range(blocks):
            for sl in range(local):
                for j in range(local):
                    message = ((d * blocks + w) * local + sl) * local + j
                    slab[message, (w * local + sl) * total + d * local + j] = 1.0
                    node[(w * total + d * local + sl) * local + j, message] = 1.0
    return slab, node


def mm(a, b):
    return jnp.dot(a, b, preferred_element_type=F32)


def split_mm(a, b):
    high = a.astype(BF16)
    low = (a - high.astype(F32)).astype(BF16)
    return mm(high, b) + mm(low, b)


def turned(chunk, index):
    return jnp.take_along_axis(chunk, index, axis=1, mode="promise_in_bounds")


def kernel(
    n, local, samples, record_len, cells,
    est_ref, rec_ref, dipr_ref, dips_ref, delay_ref, onto_ref, back_ref, swap_ref,
    to_msg_ref, from_msg_ref, to_node_ref, from_node_ref, haar_t_ref, haar_ref, scale_ref,
    out_ref,
    cur, msg_a, got_a, msg_c, got_c, msg_e, got_e, msg_rim, got_rim,
    send_sem, recv_sem,
):
    me = lax.axis_index("src")
    total = n * local
    blocks = samples // WBLK
    chunks = samples // LANES
    per = blocks * local * local
    nodes = total * local

    barrier = pltpu.get_barrier_semaphore()

    @pl.loop(1, n)
    def _(k):
        pl.semaphore_signal(
            barrier, inc=1, device_id={"src": lax.rem(me + k, n)},
            device_id_type=pl.DeviceIdType.MESH,
        )

    def remote(src, dst, it, kind, target):
        return pltpu.make_async_remote_copy(
            src_ref=src, dst_ref=dst,
            send_sem=send_sem.at[it, kind], recv_sem=recv_sem.at[it, kind],
            device_id={"src": target}, device_id_type=pl.DeviceIdType.MESH,
        )

    def landed(buf, it, kind, sems):
        whole = buf.at[it, pl.ds(0, n - 1)]
        pltpu.make_async_copy(whole, whole, sems.at[it, kind]).wait()

    delay = delay_ref[...]
    lane = lax.broadcasted_iota(jnp.int32, delay.shape, 1)
    later_index = (lane - delay) & (LANES - 1)
    earlier_index = (lane + delay) & (LANES - 1)
    from_before = lane < delay
    from_same = lane < LANES - delay
    nothing = jnp.zeros(delay.shape, F32)

    for w in range(blocks):
        for sl in range(local):
            cur[pl.ds((w * local + sl) * total, total), :] = est_ref[sl, :, w * WBLK : (w + 1) * WBLK]

    scale = scale_ref[...]
    for it in range(ITERS):
        packed = mm(to_msg_ref[...], cur[...]).astype(BF16)
        msg_a[it] = packed.reshape(n, per, WBLK)
        got_a[it, me] = msg_a[it, me]
        if it == 0:
            pl.semaphore_wait(barrier, n - 1)

        @pl.loop(1, n)
        def _(k):
            target = lax.rem(me + k, n)
            remote(msg_a.at[it, target], got_a.at[it, me], it, 0, target).start()

        landed(got_a, it, 0, recv_sem)

        ordered = mm(to_node_ref[...], got_a[it].reshape(n * per, WBLK))
        wide = [
            ordered[(c // 2) * nodes : (c // 2 + 1) * nodes, (c % 2) * LANES : (c % 2 + 1) * LANES]
            for c in range(chunks)
        ]
        moved = [turned(chunk, later_index) for chunk in wide]
        placed = [
            jnp.where(
                from_before,
                moved[c - 1] if c > 0 else nothing,
                moved[c] if c < chunks else nothing,
            ).astype(BF16)
            for c in range(chunks + 1)
        ]
        predicted = mm(onto_ref[...], jnp.concatenate(placed, axis=1))
        residual = rec_ref[...] - predicted[: rec_ref.shape[0]]
        high = residual.astype(BF16).astype(F32)
        pieces = jnp.concatenate([high, residual - high], axis=0).astype(BF16)
        picked = mm(back_ref[...], pieces)
        moved = [
            turned(picked[:, c * LANES : (c + 1) * LANES], earlier_index) for c in range(chunks + 1)
        ]
        update = [
            (wide[c] + STEP_SIZE * jnp.where(from_same, moved[c], moved[c + 1])).astype(BF16)
            for c in range(chunks)
        ]
        square = nothing
        for piece in update:
            piece = piece.astype(F32)
            square = square + piece * piece
        msg_e[it] = jnp.sum(square, axis=0, keepdims=True)
        got_e[it, me] = msg_e[it]
        update_rows = jnp.concatenate(
            [jnp.concatenate(update[2 * w : 2 * w + 2], axis=1) for w in range(blocks)], axis=0
        )
        msg_c[it] = mm(from_node_ref[...], update_rows).astype(BF16).reshape(n, per, WBLK)
        got_c[it, me] = msg_c[it, me]

        @pl.loop(1, n)
        def _(k):
            target = lax.rem(me + k, n)
            remote(msg_c.at[it, target], got_c.at[it, me], it, 1, target).start()
            remote(msg_e.at[it], got_e.at[it, me], it, 2, target).start()

        swapped = mm(swap_ref[...], update_rows)
        landed(got_c, it, 1, recv_sem)
        symmetric = (
            0.5 * (mm(from_msg_ref[...], got_c[it].reshape(n * per, WBLK)) + swapped)
        ).astype(BF16)
        for w in range(blocks):
            start = (w * local + local - 1) * total
            msg_rim[it, w] = symmetric[start : start + total]

        @pl.when(me < n - 1)
        def _():
            remote(msg_rim.at[it], got_rim.at[it], it, 3, me + 1).start()

        @pl.when(me == 0)
        def _():
            got_rim[it] = jnp.zeros(got_rim.shape[1:], BF16)

        landed(got_e, it, 2, recv_sem)
        energy = jnp.sum(got_e[it].reshape(n, LANES))
        threshold = SHRINK_RATIO * jnp.sqrt(jnp.full((1, WBLK), energy) / cells + 1e-6)

        row = lax.broadcasted_iota(jnp.int32, (total, samples), 0)
        time = lax.broadcasted_iota(jnp.int32, (total, samples), 1)

        def terms(value):
            before = jnp.where(time == 0, 0.0, pltpu.roll(value, 1, axis=1))
            after = jnp.where(time == samples - 1, 0.0, pltpu.roll(value, samples - 1, axis=1))
            return value, 0.5 * (before - after), 0.5 * (before + after) - value

        def below(value):
            return jnp.where(row == 0, 0.0, pltpu.roll(value, 1, axis=0))

        def along(parts, dip):
            value, slope, bend = parts
            return value + dip * (slope + dip * bend)

        own = [
            terms(
                jnp.concatenate(
                    [
                        symmetric[(w * local + sl) * total : (w * local + sl + 1) * total]
                        for w in range(blocks)
                    ],
                    axis=1,
                ).astype(F32)
            )
            for sl in range(local)
        ]

        for sl in reversed(range(local)):
            if sl == 0:
                @pl.when(me > 0)
                def _():
                    remote(msg_rim.at[it], got_rim.at[it], it, 3, me).wait_recv()

                prior = terms(
                    jnp.concatenate([got_rim[it, w] for w in range(blocks)], axis=1).astype(F32)
                )
            else:
                prior = own[sl - 1]
            filtered = 0.5 * own[sl][0] + 0.25 * (
                along([below(part) for part in own[sl]], dipr_ref[sl].astype(F32))
                + along(prior, dips_ref[sl].astype(F32))
            )
            rows = jnp.concatenate(
                [filtered[:, w * WBLK : (w + 1) * WBLK] for w in range(blocks)], axis=0
            )
            coeffs = split_mm(rows, haar_t_ref[...]) * scale
            shrunk = coeffs - jnp.clip(coeffs, -threshold, threshold)
            restored = split_mm(shrunk * scale, haar_ref[...]).astype(BF16)
            for w in range(blocks):
                piece = restored[w * total : (w + 1) * total]
                if it == ITERS - 1:
                    out_ref[sl, :, w * WBLK : (w + 1) * WBLK] = piece
                else:
                    cur[pl.ds((w * local + sl) * total, total), :] = piece

    for it in range(ITERS):
        landed(msg_a, it, 0, send_sem)
        landed(msg_c, it, 1, send_sem)
        landed(got_e, it, 2, send_sem)

        @pl.when(me < n - 1)
        def _():
            remote(msg_rim.at[it], got_rim.at[it], it, 3, me + 1).wait_send()


def body(n, estimate, records, dip_receiver, dip_source, delays, boat, pair):
    local, receivers, samples = estimate.shape
    total = delays.shape[0]
    record_count, local_recv, record_len = records.shape
    blocks = samples // WBLK
    cells = total * receivers * samples
    nodes = total * local
    kinds = record_count * local
    signs, scales = haar_signs(WBLK)
    slab, node = row_orders(n, local, blocks)
    me = lax.axis_index("src")

    record_rows = records.reshape(kinds, record_len).astype(F32)
    delay_rows = jnp.broadcast_to(jnp.repeat(delays, local)[:, None], (nodes, LANES))
    boat_rows = jnp.repeat(boat, local) * local + jnp.arange(nodes, dtype=jnp.int32) % local
    padded = max(16, kinds)
    onto = (jnp.arange(padded, dtype=jnp.int32)[:, None] == boat_rows[None, :]).astype(BF16)
    back = (
        boat_rows[:, None] == (jnp.arange(2 * kinds, dtype=jnp.int32) % kinds)[None, :]
    ).astype(BF16)
    local_pair = lax.dynamic_slice_in_dim(pair, me * local, local) - me * local
    place = (
        jnp.arange(blocks, dtype=jnp.int32)[:, None, None] * nodes
        + local_pair[None, :, None]
        + pair[None, None, :] * local
    ).reshape(-1)
    size = blocks * nodes
    swap = (place[:, None] == jnp.arange(size, dtype=jnp.int32)[None, :]).astype(BF16)

    per = blocks * local * local
    vmem = pl.BlockSpec(memory_space=pltpu.VMEM)
    return pl.pallas_call(
        functools.partial(kernel, n, local, samples, record_len, float(cells)),
        out_shape=jax.ShapeDtypeStruct(estimate.shape, BF16),
        in_specs=[vmem] * 15,
        out_specs=vmem,
        scratch_shapes=[
            pltpu.VMEM((size, WBLK), BF16),
            pltpu.VMEM((ITERS, n, per, WBLK), BF16),
            pltpu.VMEM((ITERS, n, per, WBLK), BF16),
            pltpu.VMEM((ITERS, n, per, WBLK), BF16),
            pltpu.VMEM((ITERS, n, per, WBLK), BF16),
            pltpu.VMEM((ITERS, 1, LANES), F32),
            pltpu.VMEM((ITERS, n, 1, LANES), F32),
            pltpu.VMEM((ITERS, blocks, total, WBLK), BF16),
            pltpu.VMEM((ITERS, blocks, total, WBLK), BF16),
            pltpu.SemaphoreType.DMA((ITERS, 4)),
            pltpu.SemaphoreType.DMA((ITERS, 4)),
        ],
        compiler_params=pltpu.CompilerParams(
            collective_id=0, has_side_effects=True, vmem_limit_bytes=48 * 1024 * 1024
        ),
    )(
        estimate, record_rows, dip_receiver, dip_source, delay_rows, onto, back, swap,
        jnp.asarray(slab, BF16), jnp.asarray(slab.T, BF16),
        jnp.asarray(node, BF16), jnp.asarray(node.T, BF16),
        jnp.asarray(signs.T, BF16), jnp.asarray(signs, BF16), jnp.asarray(scales, F32),
    )


def solution(mesh):
    return jax.shard_map(
        functools.partial(body, mesh.shape["src"]),
        mesh=mesh,
        in_specs=(
            P(("parts", "src"), None, None),
            P("parts", "src", None),
            P(("parts", "src"), None, None),
            P(("parts", "src"), None, None),
            P("parts"),
            P("parts"),
            P("parts"),
        ),
        out_specs=P(("parts", "src"), None, None),
        check_vma=False,
    )
```

time: 738 us -> 43.2 us (0.06); the launches traced: 727 us -> 42.9 us
  local copies, waits for them, and re-layouts: 322 us -> 9.87 us
  other arithmetic: 295 us -> 0.42 us
  blocking collectives: 50.2 us -> 0 us
  starting transfers between devices: 33.5 us -> 0 us
  Pallas kernels: 0 us -> 32.5 us
  waiting for transfers between devices: 20.8 us -> 0 us
    scatter x128 -> x0, other arithmetic: 288 us -> none
    gather x198 -> x0, local copies, waits for them, and re-layouts: 169 us -> none
    scatter x192 -> x0, local copies, waits for them, and re-layouts: 140 us -> none
    psum x2 -> x0, blocking collectives: 50.2 us -> none  [body(): energy = lax.psum(partial_value, 'src')]
    pallas_call x0 -> x1, Pallas kernels: none -> 32.5 us  [body(): pl.pallas_call(functools.partial(kernel, n, local, samples, record_len, f...]
    all_to_all x4 -> x0, starting transfers between devices: 29 us -> none  [the longest x2 17 us: body(): lax.all_to_all(current, 'src', split_axis=1, concat_axis=0, tiled=True)]
    all_to_all x4 -> x0, waiting for transfers between devices: 15.9 us -> none  [the longest x2 10.5 us: body(): lax.all_to_all(adjoint, 'src', split_axis=0, concat_axis=1, tiled=True)]
  transfers between devices with their start and end apart: 6 -> 0, of which waited for: 4 -> 0; matrix products, arithmetic and copies ran while one was open for 1% -> 0% of each run, Pallas kernels for 0% -> 0%
where the time goes in v1:
time: 43.2 us; the launch traced here: 42.9 us
  Pallas kernels  32.5 us (75%)
  local copies, waits for them, and re-layouts  9.87 us (23%)
    pallas_call x1, Pallas kernels, body(): pl.pallas_call(functools.partial(kernel, n, local, samples, record_len, f...  32.5 us
    unnamed x29, local copies, waits for them, and re-layouts  9.35 us

profile of v1, /device:TPU:8, one launch (start us, length us, event | category | flops | bytes accessed | tf_op | source)
XLA Modules:
  0.0 42.9 jit_solution(12679101725419987045)
XLA Ops:
  0.0 0.0 copy-start.12
  0.0 0.7 %copy-done.12 = s32[32]{0:T(128)S(1)} copy-done((s32[32]{0:T(128)S(1)}, s32[32]{0:T(128)}, u32[]{:S(2)}) %copy-start.12) | copy-done | bytes 152
  0.7 0.0 copy-start.13
  0.7 0.1 dynamic-slice_subtract_fusion
  0.7 0.6 %copy-done.13 = s32[32]{0:T(128)S(1)} copy-done((s32[32]{0:T(128)S(1)}, s32[32]{0:T(128)}, u32[]{:S(2)}) %copy-start.13) | copy-done | bytes 152
  1.3 0.1 broadcast_add_fusion.1
  1.4 0.1 broadcast_add_fusion
  1.5 0.1 add.86
  1.6 0.1 broadcast_in_dim.11
  1.6 0.0 copy-start.10
  1.6 0.1 mul.39
  1.8 0.0 copy-start.11
  1.8 0.0 copy-start.1
  1.8 0.1 compare_convert_fusion.back_ref
  1.9 0.5 %copy-done.11 = s32[32]{0:T(128)S(1)} copy-done((s32[32]{0:T(128)S(1)}, s32[32]{0:T(128)}, u32[]{:S(2)}) %copy-start.11) | copy-done | bytes 152
  2.4 0.0 copy-start
  2.4 0.1 broadcast_in_dim.8
  2.5 0.1 broadcast_in_dim.9
  2.6 0.1 broadcast_in_dim.10.delay_ref
  2.7 0.0 copy-done.10
  2.7 0.0 copy-start.9
  2.7 0.1 fusion.swap_ref
  2.8 0.0 copy-done.1
  2.8 0.5 %copy-done = bf16[2,32,1024]{2,1,0:T(8,128)(2,1)S(1)} copy-done((bf16[2,32,1024]{2,1,0:T(8,128)(2,1)S(1)}, bf16[2,32,1024]{2,1,0:T(8,128)(2,1)}, u32[]{:S(2)}) %copy-start) | copy-done | bytes 131096
  3.3 0.1 copy-done.9
  3.4 0.0 copy-start.2
  3.4 0.9 %copy-done.2 = bf16[2,32,1024]{2,1,0:T(8,128)(2,1)S(1)} copy-done((bf16[2,32,1024]{2,1,0:T(8,128)(2,1)S(1)}, bf16[2,32,1024]{2,1,0:T(8,128)(2,1)}, u32[]{:S(2)}) %copy-start.2) | copy-done | bytes 131096
  4.3 0.0 copy-start.3
  4.3 0.9 %copy-done.3 = bf16[256,256]{1,0:T(8,128)(2,1)S(1)} copy-done((bf16[256,256]{1,0:T(8,128)(2,1)S(1)}, bf16[256,256]{1,0:T(8,128)(2,1)}, u32[]{:S(2)}) %copy-start.3) | copy-done | bytes 131096
  5.2 0.0 copy-start.4
  5.2 0.9 %copy-done.4 = bf16[256,256]{1,0:T(8,128)(2,1)S(1)} copy-done((bf16[256,256]{1,0:T(8,128)(2,1)S(1)}, bf16[256,256]{1,0:T(8,128)(2,1)}, u32[]{:S(2)}) %copy-start.4) | copy-done | bytes 131096
  6.1 0.0 copy-start.5
  6.1 0.9 %copy-done.5 = bf16[256,256]{1,0:T(8,128)(2,1)S(1)} copy-done((bf16[256,256]{1,0:T(8,128)(2,1)S(1)}, bf16[256,256]{1,0:T(8,128)(2,1)}, u32[]{:S(2)}) %copy-start.5) | copy-done | bytes 131096
  7.0 0.0 copy-start.6
  7.0 0.9 %copy-done.6 = bf16[256,256]{1,0:T(8,128)(2,1)S(1)} copy-done((bf16[256,256]{1,0:T(8,128)(2,1)S(1)}, bf16[256,256]{1,0:T(8,128)(2,1)}, u32[]{:S(2)}) %copy-start.6) | copy-done | bytes 131096
  7.9 0.0 copy-start.7
  7.9 0.9 %copy-done.7 = bf16[256,256]{1,0:T(8,128)(2,1)S(1)} copy-done((bf16[256,256]{1,0:T(8,128)(2,1)S(1)}, bf16[256,256]{1,0:T(8,128)(2,1)}, u32[]{:S(2)}) %copy-start.7) | copy-done | bytes 131096
  8.8 0.0 copy-start.8
  8.8 0.9 %copy-done.8 = bf16[256,256]{1,0:T(8,128)(2,1)S(1)} copy-done((bf16[256,256]{1,0:T(8,128)(2,1)S(1)}, bf16[256,256]{1,0:T(8,128)(2,1)}, u32[]{:S(2)}) %copy-start.8) | copy-done | bytes 131096
  9.7 32.5 %shard_map.136 = bf16[2,32,1024]{2,1,0:T(8,128)(2,1)S(1)} custom-call(bf16[2,32,1024]{2,1,0:T(8,128)(2,1)S(1)} %copy-done, f32[8,1152]{1,0:T(8,128)S(1)} %reshape.98.rec_ref, bf16[2,32,1024]{2,1,0:T(8,128)(2,1)S(1)} %copy-done.1, bf16[2,32,1024]{2,1,0:T(8,128)(2,1)S(1)} %copy-done.2, s32[64,128]{1,0:T(8,128)S(1)} %broadcast_in_dim.10.delay_ref, ...), custom_call_target="tpu_custom_call" | custom-call | tf_op jit(solution)/shard_map/pallas_call | solution.py:292
  42.2 0.7 %copy.17 = bf16[2,32,1024]{2,1,0:T(8,128)(2,1)} copy(bf16[2,32,1024]{2,1,0:T(8,128)(2,1)S(1)} %shard_map.136) | data formatting | bytes 262144
  (7 shorter events, 0.0 us)
Async XLA Ops:
  0.0 0.7 %copy-start.12 = (s32[32]{0:T(128)S(1)}, s32[32]{0:T(128)}, u32[]{:S(2)}) copy-start(s32[32]{0:T(128)} %param.20) | copy-start | bytes 388
  0.7 0.7 %copy-start.13 = (s32[32]{0:T(128)S(1)}, s32[32]{0:T(128)}, u32[]{:S(2)}) copy-start(s32[32]{0:T(128)} %param.19) | copy-start | bytes 388
  1.6 1.0 %copy-start.10 = (bf16[4,2,1152]{2,1,0:T(2,128)(2,1)S(1)}, bf16[4,2,1152]{2,1,0:T(2,128)(2,1)}, u32[]{:S(2)}) copy-start(bf16[4,2,1152]{2,1,0:T(2,128)(2,1)} %param.15) | copy-start | bytes 55300
  1.8 0.7 %copy-start.11 = (s32[32]{0:T(128)S(1)}, s32[32]{0:T(128)}, u32[]{:S(2)}) copy-start(s32[32]{0:T(128)} %param.18) | copy-start | bytes 388
  1.8 1.0 %copy-start.1 = (bf16[2,32,1024]{2,1,0:T(8,128)(2,1)S(1)}, bf16[2,32,1024]{2,1,0:T(8,128)(2,1)}, u32[]{:S(2)}) copy-start(bf16[2,32,1024]{2,1,0:T(8,128)(2,1)} %dipr_ref.1) | copy-start | bytes 393220
  2.4 0.9 %copy-start = (bf16[2,32,1024]{2,1,0:T(8,128)(2,1)S(1)}, bf16[2,32,1024]{2,1,0:T(8,128)(2,1)}, u32[]{:S(2)}) copy-start(bf16[2,32,1024]{2,1,0:T(8,128)(2,1)} %est_ref.1) | copy-start | bytes 393220
  2.7 0.7 %copy-start.9 = (f32[1,256]{1,0:T(1,128)S(1)}, f32[1,256]{1,0:T(1,128)}, u32[]{:S(2)}) copy-start(f32[1,256]{1,0:T(1,128)} %constant.65.clone.scale_ref) | copy-start | bytes 3076
  3.4 0.9 %copy-start.2 = (bf16[2,32,1024]{2,1,0:T(8,128)(2,1)S(1)}, bf16[2,32,1024]{2,1,0:T(8,128)(2,1)}, u32[]{:S(2)}) copy-start(bf16[2,32,1024]{2,1,0:T(8,128)(2,1)} %dips_ref.1) | copy-start | bytes 393220
  4.3 0.9 %copy-start.3 = (bf16[256,256]{1,0:T(8,128)(2,1)S(1)}, bf16[256,256]{1,0:T(8,128)(2,1)}, u32[]{:S(2)}) copy-start(bf16[256,256]{1,0:T(8,128)(2,1)} %constant.64.clone.haar_ref) | copy-start | bytes 393220
  5.2 0.9 %copy-start.4 = (bf16[256,256]{1,0:T(8,128)(2,1)S(1)}, bf16[256,256]{1,0:T(8,128)(2,1)}, u32[]{:S(2)}) copy-start(bf16[256,256]{1,0:T(8,128)(2,1)} %constant.63.clone.haar_t_ref) | copy-start | bytes 393220
  6.1 0.9 %copy-start.5 = (bf16[256,256]{1,0:T(8,128)(2,1)S(1)}, bf16[256,256]{1,0:T(8,128)(2,1)}, u32[]{:S(2)}) copy-start(bf16[256,256]{1,0:T(8,128)(2,1)} %constant.62.clone.from_node_ref) | copy-start | bytes 393220
  7.0 0.9 %copy-start.6 = (bf16[256,256]{1,0:T(8,128)(2,1)S(1)}, bf16[256,256]{1,0:T(8,128)(2,1)}, u32[]{:S(2)}) copy-start(bf16[256,256]{1,0:T(8,128)(2,1)} %constant.61.clone.to_node_ref) | copy-start | bytes 393220
  7.9 0.9 %copy-start.7 = (bf16[256,256]{1,0:T(8,128)(2,1)S(1)}, bf16[256,256]{1,0:T(8,128)(2,1)}, u32[]{:S(2)}) copy-start(bf16[256,256]{1,0:T(8,128)(2,1)} %constant.60.clone.from_msg_ref) | copy-start | bytes 393220
  8.8 0.9 %copy-start.8 = (bf16[256,256]{1,0:T(8,128)(2,1)S(1)}, bf16[256,256]{1,0:T(8,128)(2,1)}, u32[]{:S(2)}) copy-start(bf16[256,256]{1,0:T(8,128)(2,1)} %constant.59.clone.to_msg_ref) | copy-start | bytes 393220

commit v2 on v1

--- a/solution.py
+++ b/solution.py
@@ -65,13 +65,52 @@
     return jnp.take_along_axis(chunk, index, axis=1, mode="promise_in_bounds")
 
 
+def by_row(values, rows, per_row):
+    shape = (rows, values.shape[1])
+    wanted = lax.broadcasted_iota(jnp.int32, shape, 0) // per_row
+    lane = lax.broadcasted_iota(jnp.int32, shape, 1)
+    return jnp.sum(jnp.where(lane == wanted, values, 0), axis=1, keepdims=True)
+
+
+def prepare(
+    local, total, blocks, me, rec_in, delays_ref, boat_ref, pair_ref,
+    rec_ref, delay_ref, onto_ref, back_ref, swap_ref,
+):
+    nodes = total * local
+    kinds = rec_in.shape[0] * local
+    for b in range(rec_in.shape[0]):
+        rec_ref[b * local : (b + 1) * local, :] = rec_in[b].astype(F32)
+    delay_ref[...] = jnp.broadcast_to(by_row(delays_ref[...], nodes, local), delay_ref.shape)
+    own = lax.broadcasted_iota(jnp.int32, (nodes, 1), 0) % local
+    kind = by_row(boat_ref[...], nodes, local) * local + own
+    column = lax.broadcasted_iota(jnp.int32, back_ref.shape, 1) % kinds
+    back_ref[...] = jnp.where(kind == column, 1.0, 0.0).astype(BF16)
+    column = lax.broadcasted_iota(jnp.int32, (nodes, onto_ref.shape[0]), 1)
+    onto_ref[...] = jnp.where(kind == column, 1.0, 0.0).T.astype(BF16)
+    pairs = pair_ref[...]
+    partner = by_row(pairs, total, 1) * local
+    lane = lax.broadcasted_iota(jnp.int32, pairs.shape, 1)
+    column = lax.broadcasted_iota(jnp.int32, (total, swap_ref.shape[1]), 1)
+    for sl in range(local):
+        first = me * local
+        mate = jnp.sum(jnp.where(lane == first + sl, pairs - first, 0), axis=1, keepdims=True)
+        for w in range(blocks):
+            start = (w * local + sl) * total
+            swap_ref[start : start + total, :] = jnp.where(
+                column == partner + (mate + w * nodes), 1.0, 0.0
+            ).astype(BF16)
+
+
 def kernel(
     n, local, samples, record_len, cells,
-    est_ref, rec_ref, dipr_ref, dips_ref, delay_ref, onto_ref, back_ref, swap_ref,
-    to_msg_ref, from_msg_ref, to_node_ref, from_node_ref, haar_t_ref, haar_ref, scale_ref,
+    est_hbm, rec_hbm, dipr_hbm, dips_hbm, delays_hbm, boat_hbm, pair_hbm,
+    to_msg_hbm, from_msg_hbm, to_node_hbm, from_node_hbm, haar_t_hbm, haar_hbm, scale_ref,
     out_ref,
     cur, msg_a, got_a, msg_c, got_c, msg_e, got_e, msg_rim, got_rim,
-    send_sem, recv_sem,
+    est_ref, rec_in, dipr_ref, dips_ref, delays_ref, boat_ref, pair_ref,
+    to_msg_ref, from_msg_ref, to_node_ref, from_node_ref, haar_t_ref, haar_ref,
+    rec_ref, delay_ref, onto_ref, back_ref, swap_ref,
+    send_sem, recv_sem, load_sem,
 ):
     me = lax.axis_index("src")
     total = n * local
@@ -80,6 +119,21 @@
     per = blocks * local * local
     nodes = total * local
 
+    loads = [
+        pltpu.make_async_copy(src, dst, load_sem.at[i])
+        for i, (src, dst) in enumerate(
+            [
+                (est_hbm, est_ref), (to_msg_hbm, to_msg_ref), (delays_hbm, delays_ref),
+                (boat_hbm, boat_ref), (pair_hbm, pair_ref), (rec_hbm, rec_in),
+                (to_node_hbm, to_node_ref), (from_node_hbm, from_node_ref),
+                (from_msg_hbm, from_msg_ref), (dipr_hbm, dipr_ref), (dips_hbm, dips_ref),
+                (haar_t_hbm, haar_t_ref), (haar_hbm, haar_ref),
+            ]
+        )
+    ]
+    for load in loads:
+        load.start()
+
     barrier = pltpu.get_barrier_semaphore()
 
     @pl.loop(1, n)
@@ -100,14 +154,8 @@
         whole = buf.at[it, pl.ds(0, n - 1)]
         pltpu.make_async_copy(whole, whole, sems.at[it, kind]).wait()
 
-    delay = delay_ref[...]
-    lane = lax.broadcasted_iota(jnp.int32, delay.shape, 1)
-    later_index = (lane - delay) & (LANES - 1)
-    earlier_index = (lane + delay) & (LANES - 1)
-    from_before = lane < delay
-    from_same = lane < LANES - delay
-    nothing = jnp.zeros(delay.shape, F32)
-
+    loads[0].wait()
+    loads[1].wait()
     for w in range(blocks):
         for sl in range(local):
             cur[pl.ds((w * local + sl) * total, total), :] = est_ref[sl, :, w * WBLK : (w + 1) * WBLK]
@@ -125,6 +173,21 @@
             target = lax.rem(me + k, n)
             remote(msg_a.at[it, target], got_a.at[it, me], it, 0, target).start()
 
+        if it == 0:
+            for load in loads[2:]:
+                load.wait()
+            prepare(
+                local, total, blocks, me, rec_in, delays_ref, boat_ref, pair_ref,
+                rec_ref, delay_ref, onto_ref, back_ref, swap_ref,
+            )
+
+        delay = delay_ref[...]
+        lane = lax.broadcasted_iota(jnp.int32, delay.shape, 1)
+        later_index = (lane - delay) & (LANES - 1)
+        earlier_index = (lane + delay) & (LANES - 1)
+        from_before = lane < delay
+        from_same = lane < LANES - delay
+        nothing = jnp.zeros(delay.shape, F32)
         landed(got_a, it, 0, recv_sem)
 
         ordered = mm(to_node_ref[...], got_a[it].reshape(n * per, WBLK))
@@ -268,31 +331,15 @@
     kinds = record_count * local
     signs, scales = haar_signs(WBLK)
     slab, node = row_orders(n, local, blocks)
-    me = lax.axis_index("src")
-
-    record_rows = records.reshape(kinds, record_len).astype(F32)
-    delay_rows = jnp.broadcast_to(jnp.repeat(delays, local)[:, None], (nodes, LANES))
-    boat_rows = jnp.repeat(boat, local) * local + jnp.arange(nodes, dtype=jnp.int32) % local
     padded = max(16, kinds)
-    onto = (jnp.arange(padded, dtype=jnp.int32)[:, None] == boat_rows[None, :]).astype(BF16)
-    back = (
-        boat_rows[:, None] == (jnp.arange(2 * kinds, dtype=jnp.int32) % kinds)[None, :]
-    ).astype(BF16)
-    local_pair = lax.dynamic_slice_in_dim(pair, me * local, local) - me * local
-    place = (
-        jnp.arange(blocks, dtype=jnp.int32)[:, None, None] * nodes
-        + local_pair[None, :, None]
-        + pair[None, None, :] * local
-    ).reshape(-1)
     size = blocks * nodes
-    swap = (place[:, None] == jnp.arange(size, dtype=jnp.int32)[None, :]).astype(BF16)
 
     per = blocks * local * local
     vmem = pl.BlockSpec(memory_space=pltpu.VMEM)
     return pl.pallas_call(
         functools.partial(kernel, n, local, samples, record_len, float(cells)),
         out_shape=jax.ShapeDtypeStruct(estimate.shape, BF16),
-        in_specs=[vmem] * 15,
+        in_specs=[pl.BlockSpec(memory_space=pl.ANY)] * 13 + [vmem],
         out_specs=vmem,
         scratch_shapes=[
             pltpu.VMEM((size, WBLK), BF16),
@@ -304,14 +351,34 @@
             pltpu.VMEM((ITERS, n, 1, LANES), F32),
             pltpu.VMEM((ITERS, blocks, total, WBLK), BF16),
             pltpu.VMEM((ITERS, blocks, total, WBLK), BF16),
+            pltpu.VMEM(estimate.shape, BF16),
+            pltpu.VMEM(records.shape, BF16),
+            pltpu.VMEM(estimate.shape, BF16),
+            pltpu.VMEM(estimate.shape, BF16),
+            pltpu.VMEM((1, total), jnp.int32),
+            pltpu.VMEM((1, total), jnp.int32),
+            pltpu.VMEM((1, total), jnp.int32),
+            pltpu.VMEM((size, size), BF16),
+            pltpu.VMEM((size, size), BF16),
+            pltpu.VMEM((size, size), BF16),
+            pltpu.VMEM((size, size), BF16),
+            pltpu.VMEM((WBLK, WBLK), BF16),
+            pltpu.VMEM((WBLK, WBLK), BF16),
+            pltpu.VMEM((kinds, record_len), F32),
+            pltpu.VMEM((nodes, LANES), jnp.int32),
+            pltpu.VMEM((padded, nodes), BF16),
+            pltpu.VMEM((nodes, 2 * kinds), BF16),
+            pltpu.VMEM((size, size), BF16),
             pltpu.SemaphoreType.DMA((ITERS, 4)),
             pltpu.SemaphoreType.DMA((ITERS, 4)),
+            pltpu.SemaphoreType.DMA((13,)),
         ],
         compiler_params=pltpu.CompilerParams(
-            collective_id=0, has_side_effects=True, vmem_limit_bytes=48 * 1024 * 1024
+            collective_id=0, has_side_effects=True, vmem_limit_bytes=60 * 1024 * 1024
         ),
     )(
-        estimate, record_rows, dip_receiver, dip_source, delay_rows, onto, back, swap,
+        estimate, records, dip_receiver, dip_source,
+        delays.reshape(1, total), boat.reshape(1, total), pair.reshape(1, total),
         jnp.asarray(slab, BF16), jnp.asarray(slab.T, BF16),
         jnp.asarray(node, BF16), jnp.asarray(node.T, BF16),
         jnp.asarray(signs.T, BF16), jnp.asarray(signs, BF16), jnp.asarray(scales, F32),

time: 43.2 us -> 35.7 us (0.83)
  local copies, waits for them, and re-layouts: 9.87 us -> 1.57 us
  Pallas kernels: 32.5 us -> 33.9 us
    unnamed x29 -> x1, local copies, waits for them, and re-layouts: 9.35 us -> 1.57 us
    pallas_call x1, Pallas kernels: 32.5 us -> 33.9 us  [body(): pl.pallas_call(functools.partial(kernel, n, local, samples, record_len, f...]
where the time goes in v2:
time: 35.7 us; the launch traced here: 35.5 us
  Pallas kernels  33.9 us (95%)
  local copies, waits for them, and re-layouts  1.57 us (4%)
    pallas_call x1, Pallas kernels, body(): pl.pallas_call(functools.partial(kernel, n, local, samples, record_len, f...  33.9 us
    unnamed x1, local copies, waits for them, and re-layouts  1.57 us

profile of v2, /device:TPU:8, one launch (start us, length us, event | category | flops | bytes accessed | tf_op | source)
XLA Modules:
  0.0 35.5 jit_solution(8128614457063688530)
XLA Ops:
  0.0 33.9 %shard_map.136 = bf16[2,32,1024]{2,1,0:T(8,128)(2,1)} custom-call(bf16[2,32,1024]{2,1,0:T(8,128)(2,1)} %est_hbm.1, bf16[4,2,1152]{2,1,0:T(2,128)(2,1)} %rec_hbm.1, bf16[2,32,1024]{2,1,0:T(8,128)(2,1)} %dipr_hbm.1, bf16[2,32,1024]{2,1,0:T(8,128)(2,1)} %dips_hbm.1, s32[1,32]{1,0:T(1,128)} %bitcast.3, s32[1,32]{1,0:T(1,128)} %bitcast.4, s32[1,32]{1,0:T(1,128)} %bitcast.5, ...), custom_call_target="tpu_custom_call" | custom-call | tf_op jit(solution)/shard_map/pallas_call | solution.py:339
  33.9 1.6 %copy.16 = bf16[2,32,1024]{2,1,0:T(8,128)(2,1)} copy(bf16[2,32,1024]{2,1,0:T(8,128)(2,1)} %shard_map.136) | data formatting | bytes 262144

commit v3 on v2

v3 whole, which is shorter than its diff:
```python
import functools
import math

import jax
import jax.numpy as jnp
from jax import lax
from jax.experimental import pallas as pl
from jax.experimental.pallas import tpu as pltpu
from jax.sharding import PartitionSpec as P

WBLK = 256
ITERS = 2
LANES = 128

STEP_SIZE = 0.0625
SHRINK_RATIO = 0.3

F32 = jnp.float32
BF16 = jnp.bfloat16


def one_hot(ref, column_of):
    wanted = column_of(lax.broadcasted_iota(jnp.int32, (ref.shape[0], 1), 0))
    column = lax.broadcasted_iota(jnp.int32, ref.shape, 1)
    ref[...] = jnp.where(column == wanted, 1.0, 0.0).astype(BF16)


def order_maps(n, local, blocks):
    total = n * local

    def slab_of_message(i):
        j, sl = i % local, i // local % local
        w, d = i // (local * local) % blocks, i // (local * local * blocks)
        return ((w * local + sl) * n + d) * local + j

    def message_of_slab(i):
        j, d = i % local, i // local % n
        sl, w = i // total % local, i // (total * local)
        return ((d * blocks + w) * local + sl) * local + j

    def message_of_node(i):
        sl, d = i % local, i // local % n
        j, w = i // total % local, i // (total * local)
        return ((d * blocks + w) * local + sl) * local + j

    def node_of_message(i):
        j, sl = i % local, i // local % local
        w, d = i // (local * local) % blocks, i // (local * local * blocks)
        return ((w * local + j) * n + d) * local + sl

    return slab_of_message, message_of_slab, message_of_node, node_of_message


def haar_supports(index):
    support = jnp.full(index.shape, WBLK, jnp.int32)
    first = jnp.ones(index.shape, jnp.int32)
    level = 2
    while level < WBLK:
        support = jnp.where(index >= level, WBLK // level, support)
        first = jnp.where(index >= level, level, first)
        level *= 2
    start = jnp.where(index == 0, 0, (index - first) * support)
    middle = jnp.where(index == 0, WBLK, start + support // 2)
    return start, middle, start + support


def haar_signs(ref, coefficient_axis):
    shape = (WBLK, 1) if coefficient_axis == 0 else (1, WBLK)
    start, middle, end = haar_supports(lax.broadcasted_iota(jnp.int32, shape, coefficient_axis))
    time = lax.broadcasted_iota(jnp.int32, (WBLK, WBLK), 1 - coefficient_axis)
    inside = jnp.where((time >= start) & (time < middle), 1.0, 0.0)
    ref[...] = (inside - jnp.where((time >= middle) & (time < end), 1.0, 0.0)).astype(BF16)


def haar_scales():
    index = lax.broadcasted_iota(jnp.int32, (1, WBLK), 1)
    scale = jnp.full(index.shape, 1.0 / math.sqrt(WBLK), F32)
    level = 2
    while level < WBLK:
        scale = jnp.where(index >= level, math.sqrt(level / WBLK), scale)
        level *= 2
    return scale


def mm(a, b):
    return jnp.dot(a, b, preferred_element_type=F32)


def split_mm(a, b):
    high = a.astype(BF16)
    low = (a - high.astype(F32)).astype(BF16)
    return mm(high, b) + mm(low, b)


def turned(chunk, index):
    return jnp.take_along_axis(chunk, index, axis=1, mode="promise_in_bounds")


def by_row(values, rows):
    shape = (rows, values.shape[1])
    wanted = lax.broadcasted_iota(jnp.int32, shape, 0) % values.shape[1]
    lane = lax.broadcasted_iota(jnp.int32, shape, 1)
    return jnp.sum(jnp.where(lane == wanted, values, 0), axis=1, keepdims=True)


def prepare(
    local, total, blocks, me, rec_in, delays_ref, boat_ref, pair_ref,
    rec_ref, delay_ref, onto_ref, back_ref, swap_ref, swap_msg_ref,
):
    nodes = total * local
    kinds = rec_in.shape[0] * local
    for b in range(rec_in.shape[0]):
        rec_ref[b * local : (b + 1) * local, :] = rec_in[b].astype(F32)
    delay_ref[...] = jnp.broadcast_to(by_row(delays_ref[...], nodes), delay_ref.shape)
    own = lax.broadcasted_iota(jnp.int32, (nodes, 1), 0) // total
    kind = by_row(boat_ref[...], nodes) * local + own
    column = lax.broadcasted_iota(jnp.int32, back_ref.shape, 1) % kinds
    back_ref[...] = jnp.where(kind == column, 1.0, 0.0).astype(BF16)
    column = lax.broadcasted_iota(jnp.int32, (nodes, onto_ref.shape[0]), 1)
    onto_ref[...] = jnp.where(kind == column, 1.0, 0.0).T.astype(BF16)
    pairs = pair_ref[...]
    partner = by_row(pairs, total)
    partner_msg = partner // local * (blocks * local * local) + partner % local
    lane = lax.broadcasted_iota(jnp.int32, pairs.shape, 1)
    column = lax.broadcasted_iota(jnp.int32, (total, swap_ref.shape[1]), 1)
    for sl in range(local):
        first = me * local
        mate = jnp.sum(jnp.where(lane == first + sl, pairs - first, 0), axis=1, keepdims=True)
        for w in range(blocks):
            start = (w * local + sl) * total
            swap_ref[start : start + total, :] = jnp.where(
                column == partner + (mate + w * local) * total, 1.0, 0.0
            ).astype(BF16)
            swap_msg_ref[start : start + total, :] = jnp.where(
                column == partner_msg + (mate + w * local) * local, 1.0, 0.0
            ).astype(BF16)


def by_slab(rows, at, local, total):
    count = rows.shape[0] // (local * total)
    return jnp.concatenate(
        [rows[(w * local + at) * total : (w * local + at + 1) * total] for w in range(count)],
        axis=1,
    )


def terms(value):
    samples = value.shape[1]
    time = lax.broadcasted_iota(jnp.int32, value.shape, 1)
    before = jnp.where(time == 0, 0.0, pltpu.roll(value, 1, axis=1))
    after = jnp.where(time == samples - 1, 0.0, pltpu.roll(value, samples - 1, axis=1))
    return value, 0.5 * (before - after), 0.5 * (before + after) - value


def below(value):
    row = lax.broadcasted_iota(jnp.int32, value.shape, 0)
    return jnp.where(row == 0, 0.0, pltpu.roll(value, 1, axis=0))


def along(parts, dip):
    value, slope, bend = parts
    return value + dip * (slope + dip * bend)


def kernel(
    n, local, samples, cells,
    est_hbm, rec_hbm, dipr_hbm, dips_hbm, delays_hbm, boat_hbm, pair_hbm,
    out_ref,
    cur, msg_a, got_a, msg_d, got_d, msg_c, got_c, msg_e, got_e, msg_rim, got_rim,
    est_ref, rec_in, dipr_ref, dips_ref, delays_ref, boat_ref, pair_ref,
    to_msg_ref, from_msg_ref, to_node_ref, from_node_ref, haar_t_ref, haar_ref,
    rec_ref, delay_ref, onto_ref, back_ref, swap_ref, swap_msg_ref, dip_node,
    send_sem, recv_sem, load_sem,
):
    me = lax.axis_index("src")
    total = n * local
    blocks = samples // WBLK
    chunks = samples // LANES
    per = blocks * local * local
    nodes = total * local

    barrier = pltpu.get_barrier_semaphore()

    @pl.loop(1, n)
    def _(k):
        pl.semaphore_signal(
            barrier, inc=1, device_id={"src": lax.rem(me + k, n)},
            device_id_type=pl.DeviceIdType.MESH,
        )

    loads = [
        pltpu.make_async_copy(src, dst, load_sem.at[i])
        for i, (src, dst) in enumerate(
            [
                (est_hbm, est_ref), (dipr_hbm, dipr_ref), (dips_hbm, dips_ref),
                (delays_hbm, delays_ref), (boat_hbm, boat_ref), (pair_hbm, pair_ref),
                (rec_hbm, rec_in),
            ]
        )
    ]
    for load in loads:
        load.start()

    def remote(src, dst, it, kind, target):
        return pltpu.make_async_remote_copy(
            src_ref=src, dst_ref=dst,
            send_sem=send_sem.at[it, kind], recv_sem=recv_sem.at[it, kind],
            device_id={"src": target}, device_id_type=pl.DeviceIdType.MESH,
        )

    def landed(buf, it, kind, sems):
        whole = buf.at[pl.ds(0, n - 1)]
        pltpu.make_async_copy(whole, whole, sems.at[it, kind]).wait()

    slab_of_message, message_of_slab, message_of_node, node_of_message = order_maps(
        n, local, blocks
    )
    one_hot(to_msg_ref, slab_of_message)

    def packed(ref):
        rows = jnp.concatenate(
            [
                ref[sl, :, w * WBLK : (w + 1) * WBLK]
                for w in range(blocks)
                for sl in range(local)
            ],
            axis=0,
        )
        return mm(to_msg_ref[...], rows).astype(BF16).reshape(n, per, WBLK)

    loads[0].wait()
    msg_a[...] = packed(est_ref)
    got_a[me] = msg_a[me]
    loads[1].wait()
    loads[2].wait()
    msg_d[:, :per, :] = packed(dipr_ref)
    msg_d[:, per:, :] = packed(dips_ref)
    got_d[me] = msg_d[me]
    pl.semaphore_wait(barrier, n - 1)

    @pl.loop(1, n)
    def _(k):
        target = lax.rem(me + n - k, n)
        remote(msg_a.at[target], got_a.at[me], 0, 0, target).start()

    @pl.loop(1, n)
    def _(k):
        target = lax.rem(me + n - k, n)
        remote(msg_d.at[target], got_d.at[me], 0, 4, target).start()

    for load in loads[3:]:
        load.wait()
    one_hot(to_node_ref, message_of_node)
    prepare(
        local, total, blocks, me, rec_in, delays_ref, boat_ref, pair_ref,
        rec_ref, delay_ref, onto_ref, back_ref, swap_ref, swap_msg_ref,
    )
    one_hot(from_node_ref, node_of_message)
    one_hot(from_msg_ref, message_of_slab)
    haar_signs(haar_t_ref, 1)
    haar_signs(haar_ref, 0)
    scale = haar_scales()

    landed(got_a, 0, 0, recv_sem)
    cur[...] = mm(to_node_ref[...], got_a[...].reshape(n * per, WBLK))

    for it in range(ITERS):
        last = it == ITERS - 1
        delay = delay_ref[...]
        lane = lax.broadcasted_iota(jnp.int32, delay.shape, 1)
        later_index = (lane - delay) & (LANES - 1)
        earlier_index = (lane + delay) & (LANES - 1)
        from_before = lane < delay
        from_same = lane < LANES - delay
        nothing = jnp.zeros(delay.shape, F32)
        wide = [
            cur[(c // 2) * nodes : (c // 2 + 1) * nodes, (c % 2) * LANES : (c % 2 + 1) * LANES]
            for c in range(chunks)
        ]
        moved = [turned(chunk, later_index) for chunk in wide]
        placed = [
            jnp.where(
                from_before,
                moved[c - 1] if c > 0 else nothing,
                moved[c] if c < chunks else nothing,
            ).astype(BF16)
            for c in range(chunks + 1)
        ]
        predicted = mm(onto_ref[...], jnp.concatenate(placed, axis=1))
        residual = rec_ref[...] - predicted[: rec_ref.shape[0]]
        high = residual.astype(BF16).astype(F32)
        pieces = jnp.concatenate([high, residual - high], axis=0).astype(BF16)
        picked = mm(back_ref[...], pieces)
        moved = [
            turned(picked[:, c * LANES : (c + 1) * LANES], earlier_index) for c in range(chunks + 1)
        ]
        update = [
            (wide[c] + STEP_SIZE * jnp.where(from_same, moved[c], moved[c + 1])).astype(BF16)
            for c in range(chunks)
        ]
        update_rows = jnp.concatenate(
            [jnp.concatenate(update[2 * w : 2 * w + 2], axis=1) for w in range(blocks)], axis=0
        )
        msg_c[it] = mm(from_node_ref[...], update_rows).astype(BF16).reshape(n, per, WBLK)

        @pl.loop(1, n)
        def _(k):
            target = lax.rem(me + n - k, n)
            remote(msg_c.at[it, target], got_c.at[it, me], it, 1, target).start()

        square = nothing
        for piece in update:
            piece = piece.astype(F32)
            square = square + piece * piece
        msg_e[it] = jnp.sum(square, axis=0, keepdims=True)

        @pl.loop(1, n)
        def _(k):
            target = lax.rem(me + n - k, n)
            remote(msg_e.at[it], got_e.at[it, me], it, 2, target).start()

        got_e[it, me] = msg_e[it]
        got_c[it, me] = msg_c[it, me]

        if not last:
            landed(got_d, 0, 4, recv_sem)
            for i in range(2):
                rows = got_d[:, i * per : (i + 1) * per, :].reshape(n * per, WBLK)
                dip_node[i] = mm(to_node_ref[...], rows).astype(BF16)
            kept = update_rows.astype(F32)
        else:
            kept = mm(swap_ref[...], update_rows)
        arrange = from_msg_ref if last else swap_msg_ref
        landed(got_c.at[it], it, 1, recv_sem)
        symmetric = (
            0.5 * (mm(arrange[...], got_c[it].reshape(n * per, WBLK)) + kept)
        ).astype(BF16)
        for w in range(blocks):
            start = (w * local + local - 1) * total
            msg_rim[it, w] = symmetric[start : start + total]

        @pl.when(me < n - 1)
        def _():
            remote(msg_rim.at[it], got_rim.at[it], it, 3, me + 1).start()

        @pl.when(me == 0)
        def _():
            got_rim[it] = jnp.zeros(got_rim.shape[1:], BF16)

        own = [terms(by_slab(symmetric, at, local, total).astype(F32)) for at in range(local)]

        landed(got_e.at[it], it, 2, recv_sem)
        energy = jnp.sum(got_e[it].reshape(n, LANES))
        threshold = SHRINK_RATIO * jnp.sqrt(jnp.full((1, WBLK), energy) / cells + 1e-6)

        for at in reversed(range(local)):
            if last:
                within, across = dipr_ref[at], dips_ref[at]
            else:
                within = by_slab(dip_node[1], at, local, total)
                across = by_slab(dip_node[0], at, local, total)
            inside = along([below(part) for part in own[at]], within.astype(F32))
            if at == 0:
                @pl.when(me > 0)
                def _():
                    remote(msg_rim.at[it], got_rim.at[it], it, 3, me).wait_recv()

                prior = terms(
                    jnp.concatenate([got_rim[it, w] for w in range(blocks)], axis=1).astype(F32)
                )
            else:
                prior = own[at - 1]
            filtered = 0.5 * own[at][0] + 0.25 * (inside + along(prior, across.astype(F32)))
            rows = jnp.concatenate(
                [filtered[:, w * WBLK : (w + 1) * WBLK] for w in range(blocks)], axis=0
            )
            coeffs = split_mm(rows, haar_t_ref[...]) * scale
            shrunk = coeffs - jnp.clip(coeffs, -threshold, threshold)
            restored = split_mm(shrunk * scale, haar_ref[...]).astype(BF16)
            for w in range(blocks):
                piece = restored[w * total : (w + 1) * total]
                if last:
                    out_ref[at, :, w * WBLK : (w + 1) * WBLK] = piece
                else:
                    start = (w * local + at) * total
                    cur[start : start + total, :] = piece.astype(F32)

    landed(msg_a, 0, 0, send_sem)
    landed(msg_d, 0, 4, send_sem)
    for it in range(ITERS):
        landed(msg_c.at[it], it, 1, send_sem)
        landed(got_e.at[it], it, 2, send_sem)

        @pl.when(me < n - 1)
        def _():
            remote(msg_rim.at[it], got_rim.at[it], it, 3, me + 1).wait_send()


def body(n, estimate, records, dip_receiver, dip_source, delays, boat, pair):
    local, receivers, samples = estimate.shape
    total = delays.shape[0]
    record_count, local_recv, record_len = records.shape
    blocks = samples // WBLK
    cells = total * receivers * samples
    nodes = total * local
    kinds = record_count * local
    padded = max(16, kinds)
    size = blocks * nodes

    per = blocks * local * local
    vmem = pl.BlockSpec(memory_space=pltpu.VMEM)
    return pl.pallas_call(
        functools.partial(kernel, n, local, samples, float(cells)),
        out_shape=jax.ShapeDtypeStruct(estimate.shape, BF16),
        in_specs=[pl.BlockSpec(memory_space=pl.ANY)] * 7,
        out_specs=vmem,
        scratch_shapes=[
            pltpu.VMEM((size, WBLK), F32),
            pltpu.VMEM((n, per, WBLK), BF16),
            pltpu.VMEM((n, per, WBLK), BF16),
            pltpu.VMEM((n, 2 * per, WBLK), BF16),
            pltpu.VMEM((n, 2 * per, WBLK), BF16),
            pltpu.VMEM((ITERS, n, per, WBLK), BF16),
            pltpu.VMEM((ITERS, n, per, WBLK), BF16),
            pltpu.VMEM((ITERS, 1, LANES), F32),
            pltpu.VMEM((ITERS, n, 1, LANES), F32),
            pltpu.VMEM((ITERS, blocks, total, WBLK), BF16),
            pltpu.VMEM((ITERS, blocks, total, WBLK), BF16),
            pltpu.VMEM(estimate.shape, BF16),
            pltpu.VMEM(records.shape, BF16),
            pltpu.VMEM(estimate.shape, BF16),
            pltpu.VMEM(estimate.shape, BF16),
            pltpu.VMEM((1, total), jnp.int32),
            pltpu.VMEM((1, total), jnp.int32),
            pltpu.VMEM((1, total), jnp.int32),
            pltpu.VMEM((size, size), BF16),
            pltpu.VMEM((size, size), BF16),
            pltpu.VMEM((size, size), BF16),
            pltpu.VMEM((size, size), BF16),
            pltpu.VMEM((WBLK, WBLK), BF16),
            pltpu.VMEM((WBLK, WBLK), BF16),
            pltpu.VMEM((kinds, record_len), F32),
            pltpu.VMEM((nodes, LANES), jnp.int32),
            pltpu.VMEM((padded, nodes), BF16),
            pltpu.VMEM((nodes, 2 * kinds), BF16),
            pltpu.VMEM((size, size), BF16),
            pltpu.VMEM((size, size), BF16),
            pltpu.VMEM((2, size, WBLK), BF16),
            pltpu.SemaphoreType.DMA((ITERS, 5)),
            pltpu.SemaphoreType.DMA((ITERS, 5)),
            pltpu.SemaphoreType.DMA((7,)),
        ],
        compiler_params=pltpu.CompilerParams(
            collective_id=0, has_side_effects=True, vmem_limit_bytes=60 * 1024 * 1024
        ),
    )(
        estimate, records, dip_receiver, dip_source,
        delays.reshape(1, total), boat.reshape(1, total), pair.reshape(1, total),
    )


def solution(mesh):
    return jax.shard_map(
        functools.partial(body, mesh.shape["src"]),
        mesh=mesh,
        in_specs=(
            P(("parts", "src"), None, None),
            P("parts", "src", None),
            P(("parts", "src"), None, None),
            P(("parts", "src"), None, None),
            P("parts"),
            P("parts"),
            P("parts"),
        ),
        out_specs=P(("parts", "src"), None, None),
        check_vma=False,
    )
```

time: 35.7 us -> 32.3 us (0.905)
  Pallas kernels: 33.9 us -> 30.6 us
    pallas_call x1, Pallas kernels: 33.9 us -> 30.6 us  [body(): pl.pallas_call(functools.partial(kernel, n, local, samples, float(cells))...]
where the time goes in v3:
time: 32.3 us; the launch traced here: 32.2 us
  Pallas kernels  30.6 us (95%)
  local copies, waits for them, and re-layouts  1.57 us (5%)
    pallas_call x1, Pallas kernels, body(): pl.pallas_call(functools.partial(kernel, n, local, samples, float(cells))...  30.6 us
    unnamed x1, local copies, waits for them, and re-layouts  1.57 us

profile of v3, /device:TPU:8, one launch (start us, length us, event | category | flops | bytes accessed | tf_op | source)
XLA Modules:
  0.0 32.2 jit_solution(15240064495519059468)
XLA Ops:
  0.0 30.6 %shard_map.73 = bf16[2,32,1024]{2,1,0:T(8,128)(2,1)} custom-call(bf16[2,32,1024]{2,1,0:T(8,128)(2,1)} %est_hbm.1, bf16[4,2,1152]{2,1,0:T(2,128)(2,1)} %rec_hbm.1, bf16[2,32,1024]{2,1,0:T(8,128)(2,1)} %dipr_hbm.1, bf16[2,32,1024]{2,1,0:T(8,128)(2,1)} %dips_hbm.1, s32[1,32]{1,0:T(1,128)} %bitcast.3, s32[1,32]{1,0:T(1,128)} %bitcast.4, s32[1,32]{1,0:T(1,128)} %bitcast.5), custom_call_target="tpu_custom_call" | custom-call | tf_op jit(solution)/shard_map/pallas_call | solution.py:412
  30.6 1.6 %copy.9 = bf16[2,32,1024]{2,1,0:T(8,128)(2,1)} copy(bf16[2,32,1024]{2,1,0:T(8,128)(2,1)} %shard_map.73) | data formatting | bytes 262144

commit v4 on v3

--- a/solution.py
+++ b/solution.py
@@ -181,10 +181,14 @@
 
     barrier = pltpu.get_barrier_semaphore()
 
-    @pl.loop(1, n)
-    def _(k):
+    bits = [me // 2**i % 2 for i in range(n.bit_length() - 1)]
+
+    def partner_at(k):
+        return sum((1 - bit if k >> i & 1 else bit) * 2**i for i, bit in enumerate(bits))
+
+    for k in reversed(range(1, n)):
         pl.semaphore_signal(
-            barrier, inc=1, device_id={"src": lax.rem(me + k, n)},
+            barrier, inc=1, device_id={"src": partner_at(k)},
             device_id_type=pl.DeviceIdType.MESH,
         )
 
@@ -238,15 +242,9 @@
     got_d[me] = msg_d[me]
     pl.semaphore_wait(barrier, n - 1)
 
-    @pl.loop(1, n)
-    def _(k):
-        target = lax.rem(me + n - k, n)
+    for k in reversed(range(1, n)):
+        target = partner_at(k)
         remote(msg_a.at[target], got_a.at[me], 0, 0, target).start()
-
-    @pl.loop(1, n)
-    def _(k):
-        target = lax.rem(me + n - k, n)
-        remote(msg_d.at[target], got_d.at[me], 0, 4, target).start()
 
     for load in loads[3:]:
         load.wait()
@@ -260,6 +258,12 @@
     haar_signs(haar_t_ref, 1)
     haar_signs(haar_ref, 0)
     scale = haar_scales()
+
+    landed(msg_a, 0, 0, send_sem)
+
+    for k in reversed(range(1, n)):
+        target = partner_at(k)
+        remote(msg_d.at[target], got_d.at[me], 0, 4, target).start()
 
     landed(got_a, 0, 0, recv_sem)
     cur[...] = mm(to_node_ref[...], got_a[...].reshape(n * per, WBLK))
@@ -303,9 +307,8 @@
         )
         msg_c[it] = mm(from_node_ref[...], update_rows).astype(BF16).reshape(n, per, WBLK)
 
-        @pl.loop(1, n)
-        def _(k):
-            target = lax.rem(me + n - k, n)
+        for k in reversed(range(1, n)):
+            target = partner_at(k)
             remote(msg_c.at[it, target], got_c.at[it, me], it, 1, target).start()
 
         square = nothing
@@ -314,9 +317,8 @@
             square = square + piece * piece
         msg_e[it] = jnp.sum(square, axis=0, keepdims=True)
 
-        @pl.loop(1, n)
-        def _(k):
-            target = lax.rem(me + n - k, n)
+        for k in reversed(range(1, n)):
+            target = partner_at(k)
             remote(msg_e.at[it], got_e.at[it, me], it, 2, target).start()
 
         got_e[it, me] = msg_e[it]
@@ -385,7 +387,6 @@
                     start = (w * local + at) * total
                     cur[start : start + total, :] = piece.astype(F32)
 
-    landed(msg_a, 0, 0, send_sem)
     landed(msg_d, 0, 4, send_sem)
     for it in range(ITERS):
         landed(msg_c.at[it], it, 1, send_sem)

time: 32.3 us -> 31.9 us (0.988); the launches traced: 32.2 us -> 31.4 us
  Pallas kernels: 30.6 us -> 29.8 us
    pallas_call x1, Pallas kernels: 30.6 us -> 29.8 us  [body(): pl.pallas_call(functools.partial(kernel, n, local, samples, float(cells))...]
where the time goes in v4:
time: 31.9 us; the launch traced here: 31.4 us
  Pallas kernels  29.8 us (93%)
  local copies, waits for them, and re-layouts  1.57 us (5%)
    pallas_call x1, Pallas kernels, body(): pl.pallas_call(functools.partial(kernel, n, local, samples, float(cells))...  29.8 us
    unnamed x1, local copies, waits for them, and re-layouts  1.57 us

profile of v4, /device:TPU:8, one launch (start us, length us, event | category | flops | bytes accessed | tf_op | source)
XLA Modules:
  0.0 31.4 jit_solution(16868371867012735705)
XLA Ops:
  0.0 29.8 %shard_map.73 = bf16[2,32,1024]{2,1,0:T(8,128)(2,1)} custom-call(bf16[2,32,1024]{2,1,0:T(8,128)(2,1)} %est_hbm.1, bf16[4,2,1152]{2,1,0:T(2,128)(2,1)} %rec_hbm.1, bf16[2,32,1024]{2,1,0:T(8,128)(2,1)} %dipr_hbm.1, bf16[2,32,1024]{2,1,0:T(8,128)(2,1)} %dips_hbm.1, s32[1,32]{1,0:T(1,128)} %bitcast.3, s32[1,32]{1,0:T(1,128)} %bitcast.4, s32[1,32]{1,0:T(1,128)} %bitcast.5), custom_call_target="tpu_custom_call" | custom-call | tf_op jit(solution)/shard_map/pallas_call | solution.py:413
  29.8 1.6 %copy.9 = bf16[2,32,1024]{2,1,0:T(8,128)(2,1)} copy(bf16[2,32,1024]{2,1,0:T(8,128)(2,1)} %shard_map.73) | data formatting | bytes 262144

commit v5 on v4

--- a/solution.py
+++ b/solution.py
@@ -334,12 +334,16 @@
             kept = mm(swap_ref[...], update_rows)
         arrange = from_msg_ref if last else swap_msg_ref
         landed(got_c.at[it], it, 1, recv_sem)
-        symmetric = (
-            0.5 * (mm(arrange[...], got_c[it].reshape(n * per, WBLK)) + kept)
-        ).astype(BF16)
-        for w in range(blocks):
-            start = (w * local + local - 1) * total
-            msg_rim[it, w] = symmetric[start : start + total]
+        arrived = got_c[it].reshape(n * per, WBLK)
+
+        def symmetric(at):
+            starts = [(w * local + at) * total for w in range(blocks)]
+            table = jnp.concatenate([arrange[i : i + total, :] for i in starts], axis=0)
+            here = jnp.concatenate([kept[i : i + total] for i in starts], axis=0)
+            return (0.5 * (mm(table, arrived) + here)).astype(BF16)
+
+        edge = symmetric(local - 1)
+        msg_rim[it] = edge.reshape(blocks, total, WBLK)
 
         @pl.when(me < n - 1)
         def _():
@@ -349,7 +353,8 @@
         def _():
             got_rim[it] = jnp.zeros(got_rim.shape[1:], BF16)
 
-        own = [terms(by_slab(symmetric, at, local, total).astype(F32)) for at in range(local)]
+        slabs = [symmetric(at) for at in range(local - 1)] + [edge]
+        own = [terms(by_slab(slab, 0, 1, total).astype(F32)) for slab in slabs]
 
         landed(got_e.at[it], it, 2, recv_sem)
         energy = jnp.sum(got_e[it].reshape(n, LANES))

time: 31.9 us -> 31.9 us (level)
  no operation moved by 1% of the time
where the time goes in v5:
time: 31.9 us; the launch traced here: 31.3 us
  Pallas kernels  29.7 us (93%)
  local copies, waits for them, and re-layouts  1.57 us (5%)
    pallas_call x1, Pallas kernels, body(): pl.pallas_call(functools.partial(kernel, n, local, samples, float(cells))...  29.7 us
    unnamed x1, local copies, waits for them, and re-layouts  1.57 us

profile of v5, /device:TPU:8, one launch (start us, length us, event | category | flops | bytes accessed | tf_op | source)
XLA Modules:
  0.0 31.3 jit_solution(1642861591166924277)
XLA Ops:
  0.0 29.7 %shard_map.73 = bf16[2,32,1024]{2,1,0:T(8,128)(2,1)} custom-call(bf16[2,32,1024]{2,1,0:T(8,128)(2,1)} %est_hbm.1, bf16[4,2,1152]{2,1,0:T(2,128)(2,1)} %rec_hbm.1, bf16[2,32,1024]{2,1,0:T(8,128)(2,1)} %dipr_hbm.1, bf16[2,32,1024]{2,1,0:T(8,128)(2,1)} %dips_hbm.1, s32[1,32]{1,0:T(1,128)} %bitcast.3, s32[1,32]{1,0:T(1,128)} %bitcast.4, s32[1,32]{1,0:T(1,128)} %bitcast.5), custom_call_target="tpu_custom_call" | custom-call | tf_op jit(solution)/shard_map/pallas_call | solution.py:418
  29.7 1.6 %copy.9 = bf16[2,32,1024]{2,1,0:T(8,128)(2,1)} copy(bf16[2,32,1024]{2,1,0:T(8,128)(2,1)} %shard_map.73) | data formatting | bytes 262144
